TPU v7x, 256 devices: a whole 4x4x8 slice. The times are simulated.
256 devices in a mesh: gen: 32 (over y, x, core), beam: 8 (over z).
Axes of the slice: x: 4, y: 4, z: 8, core: 2. Of those that a mesh axis runs over, the one named last changes fastest.
Arguments:
- gen_showers: bfloat16 [32768, 256], P('gen'), may hold values from -12 to 12
- beam_showers: bfloat16 [16384, 256], P('beam'), may hold values from -6 to 6
- embed_weight: bfloat16 [256, 128], replicated, may hold values from -0.375 to 0.375
- eps_roster: float32 [4], replicated, may hold values from 0.04 to 0.08
Outputs:
- gen_potential: float32 [32768], P('gen')
- beam_potential: float32 [16384], P('beam')
- weight_grad: float32 [256, 128], replicated
All inputs are finite; a program needn't handle non-finite values.
Results may differ from a plain program's by a relative error of at most 0.03.
Values sent between devices are 32-bit elements; how exact they have to be, the bound alone decides.
No kernel may reach another device: no remote copies, remote signals or barrier semaphores. Data moves between devices by JAX's collectives and lax.ppermute only.
A program may use at most 64 MiB of HBM per device.

v0:
```python
import math
import jax
import jax.numpy as jnp
from jax import lax
from jax.sharding import PartitionSpec as P

SWEEPS = 4


def embed(showers, weight):
    act = jnp.tanh(jnp.dot(showers, weight, preferred_element_type=jnp.float32))
    return (act, act.astype(jnp.bfloat16))


def tile_cost(gen_emb, beam_emb, gen_sq, beam_sq):
    cross = lax.dot_general(
        gen_emb, beam_emb, (((1,), (1,)), ((), ())), preferred_element_type=jnp.float32
    )
    return gen_sq[:, None] + beam_sq[None, :] - 2.0 * cross


def row_lse(scores):
    top = lax.pmax(jnp.max(scores, axis=1), "beam")
    total = lax.psum(jnp.sum(jnp.exp(scores - top[:, None]), axis=1), "beam")
    return top + jnp.log(total)


def col_lse(scores):
    top = lax.pmax(jnp.max(scores, axis=0), "gen")
    total = lax.psum(jnp.sum(jnp.exp(scores - top[None, :]), axis=0), "gen")
    return top + jnp.log(total)


def transpose_dot(left, right):
    return lax.dot_general(
        left.astype(jnp.float32),
        right,
        (((0,), (0,)), ((), ())),
        precision=lax.Precision.HIGHEST,
        preferred_element_type=jnp.float32,
    )


def on_device(gen_showers, beam_showers, embed_weight, eps_roster):
    gen_act, gen_emb = embed(gen_showers, embed_weight)
    beam_act, beam_emb = embed(beam_showers, embed_weight)
    gen_float = gen_emb.astype(jnp.float32)
    beam_float = beam_emb.astype(jnp.float32)
    gen_sq = jnp.sum(gen_float * gen_float, axis=1)
    beam_sq = jnp.sum(beam_float * beam_float, axis=1)
    rows = gen_emb.shape[0]
    columns = beam_emb.shape[0]
    log_beam = math.log(columns * lax.axis_size("beam"))
    log_gen = math.log(rows * lax.axis_size("gen"))
    beam_pot = jnp.zeros((columns,), jnp.float32)
    gen_pot = jnp.zeros((rows,), jnp.float32)
    for sweep in range(SWEEPS):
        temper = eps_roster[sweep]
        cost = tile_cost(gen_emb, beam_emb, gen_sq, beam_sq)
        gen_pot = temper * (log_beam - row_lse((beam_pot[None, :] - cost) / temper))
        cost = tile_cost(gen_emb, beam_emb, gen_sq, beam_sq)
        beam_pot = temper * (log_gen - col_lse((gen_pot[:, None] - cost) / temper))
    last = eps_roster[SWEEPS - 1]
    cost = tile_cost(gen_emb, beam_emb, gen_sq, beam_sq)
    mass = jnp.exp((gen_pot[:, None] + beam_pot[None, :] - cost) / last - log_beam)
    plan = mass.astype(jnp.bfloat16)
    gen_count = rows // lax.axis_size("beam")
    part = plan
    row_mass = jnp.sum(mass, axis=1)
    own = gen_float
    moved = jnp.dot(part, beam_emb, preferred_element_type=jnp.float32)
    grad_gen = lax.psum_scatter(
        2.0 * (row_mass[:, None] * own - moved), "beam", scatter_dimension=0, tiled=True
    )
    gen_start = lax.axis_index("beam") * gen_count
    act_rows = lax.dynamic_slice_in_dim(gen_act, gen_start, gen_count, 0)
    shower_rows = lax.dynamic_slice_in_dim(gen_showers, gen_start, gen_count, 0)
    beam_count = columns // lax.axis_size("gen")
    part = plan
    col_mass = jnp.sum(mass, axis=0)
    own = beam_float
    moved = lax.dot_general(
        part, gen_emb, (((0,), (0,)), ((), ())), preferred_element_type=jnp.float32
    )
    grad_beam = lax.psum_scatter(
        2.0 * (col_mass[:, None] * own - moved), "gen", scatter_dimension=0, tiled=True
    )
    beam_start = lax.axis_index("gen") * beam_count
    act_cols = lax.dynamic_slice_in_dim(beam_act, beam_start, beam_count, 0)
    shower_cols = lax.dynamic_slice_in_dim(beam_showers, beam_start, beam_count, 0)
    partial_grad = transpose_dot(shower_rows, grad_gen * (1.0 - act_rows * act_rows))
    partial_grad = partial_grad + transpose_dot(
        shower_cols, grad_beam * (1.0 - act_cols * act_cols)
    )
    weight_grad = lax.psum(partial_grad, ("gen", "beam"))
    return (gen_pot, beam_pot, weight_grad)


def solution(mesh):
    in_specs = (P("gen", None), P("beam", None), P(), P())
    out_specs = (P("gen"), P("beam"), P())
    return jax.shard_map(
        on_device, mesh=mesh, in_specs=in_specs, out_specs=out_specs, check_vma=False
    )
```

profile of v0, /device:TPU:8, one launch (start us, length us, event | category | flops | bytes accessed | tf_op | source)
XLA Modules:
  0.0 1114.6 jit_solution(14821040143072383777)
XLA Ops:
  11.4 5.3 fusion
  16.7 20.0 %pmax.56 = f32[1024]{0:T(1024)S(1)} all-reduce(f32[1024]{0:T(1024)S(1)} %get-tuple-element.16), channel_id=1, replica_groups=mesh['gen'=32,'beam'=8] {'beam'}, use_global_device_ids=true, to_apply=%region_3.0 | all-reduce | flops 1024 | bytes 8192 | tf_op jit(solution)/shard_map/pmax | solution.py:23
  36.7 5.1 exponential_reduce_fusion.7
  41.8 14.2 %psum.63 = f32[1024]{0:T(1024)S(1)} all-reduce(f32[1024]{0:T(1024)S(1)} %exponential_reduce_fusion.7), channel_id=1, replica_groups=mesh['gen'=32,'beam'=8] {'beam'}, use_global_device_ids=true, to_apply=%region_5.0 | all-reduce | flops 1024 | bytes 8192 | tf_op jit(solution)/shard_map/psum | solution.py:24
  61.3 54.0 %pmax.57 = f32[2048]{0:T(1024)S(1)} all-reduce(f32[2048]{0:T(1024)S(1)} %fusion.15), channel_id=1, replica_groups=mesh['gen'=32,'beam'=8] {'gen'}, use_global_device_ids=true, to_apply=%region_7.0 | all-reduce | flops 2048 | bytes 16384 | tf_op jit(solution)/shard_map/pmax | solution.py:29
  115.4 5.2 exponential_reduce_fusion.6
  120.5 55.5 %psum.64 = f32[2048]{0:T(1024)S(1)} all-reduce(f32[2048]{0:T(1024)S(1)} %exponential_reduce_fusion.6), channel_id=1, replica_groups=mesh['gen'=32,'beam'=8] {'gen'}, use_global_device_ids=true, to_apply=%region_9.0 | all-reduce | flops 2048 | bytes 16384 | tf_op jit(solution)/shard_map/psum | solution.py:30
  176.7 4.8 fusion.1
  181.5 16.2 %pmax.58 = f32[1024]{0:T(1024)S(1)} all-reduce(f32[1024]{0:T(1024)S(1)} %fusion.1), channel_id=1, replica_groups=mesh['gen'=32,'beam'=8] {'beam'}, use_global_device_ids=true, to_apply=%region_11.0 | all-reduce | flops 1024 | bytes 8192 | tf_op jit(solution)/shard_map/pmax | solution.py:23
  197.7 5.1 exponential_reduce_fusion.5
  202.8 14.2 %psum.65 = f32[1024]{0:T(1024)S(1)} all-reduce(f32[1024]{0:T(1024)S(1)} %exponential_reduce_fusion.5), channel_id=1, replica_groups=mesh['gen'=32,'beam'=8] {'beam'}, use_global_device_ids=true, to_apply=%region_13.0 | all-reduce | flops 1024 | bytes 8192 | tf_op jit(solution)/shard_map/psum | solution.py:24
  222.1 63.7 %pmax.59 = f32[2048]{0:T(1024)S(1)} all-reduce(f32[2048]{0:T(1024)S(1)} %fusion.16), channel_id=1, replica_groups=mesh['gen'=32,'beam'=8] {'gen'}, use_global_device_ids=true, to_apply=%region_15.0 | all-reduce | flops 2048 | bytes 16384 | tf_op jit(solution)/shard_map/pmax | solution.py:29
  285.8 5.1 exponential_reduce_fusion.4
  290.9 63.7 %psum.66 = f32[2048]{0:T(1024)S(1)} all-reduce(f32[2048]{0:T(1024)S(1)} %exponential_reduce_fusion.4), channel_id=1, replica_groups=mesh['gen'=32,'beam'=8] {'gen'}, use_global_device_ids=true, to_apply=%region_17.0 | all-reduce | flops 2048 | bytes 16384 | tf_op jit(solution)/shard_map/psum | solution.py:30
  355.2 4.9 fusion.2
  360.1 16.2 %pmax.60 = f32[1024]{0:T(1024)S(1)} all-reduce(f32[1024]{0:T(1024)S(1)} %fusion.2), channel_id=1, replica_groups=mesh['gen'=32,'beam'=8] {'beam'}, use_global_device_ids=true, to_apply=%region_19.0 | all-reduce | flops 1024 | bytes 8192 | tf_op jit(solution)/shard_map/pmax | solution.py:23
  376.3 5.1 exponential_reduce_fusion.3
  381.4 14.3 %psum.67 = f32[1024]{0:T(1024)S(1)} all-reduce(f32[1024]{0:T(1024)S(1)} %exponential_reduce_fusion.3), channel_id=1, replica_groups=mesh['gen'=32,'beam'=8] {'beam'}, use_global_device_ids=true, to_apply=%region_21.0 | all-reduce | flops 1024 | bytes 8192 | tf_op jit(solution)/shard_map/psum | solution.py:24
  401.1 63.7 %pmax.61 = f32[2048]{0:T(1024)S(1)} all-reduce(f32[2048]{0:T(1024)S(1)} %fusion.17), channel_id=1, replica_groups=mesh['gen'=32,'beam'=8] {'gen'}, use_global_device_ids=true, to_apply=%region_23.0 | all-reduce | flops 2048 | bytes 16384 | tf_op jit(solution)/shard_map/pmax | solution.py:29
  464.8 5.2 exponential_reduce_fusion.2
  470.0 63.7 %psum.68 = f32[2048]{0:T(1024)S(1)} all-reduce(f32[2048]{0:T(1024)S(1)} %exponential_reduce_fusion.2), channel_id=1, replica_groups=mesh['gen'=32,'beam'=8] {'gen'}, use_global_device_ids=true, to_apply=%region_25.0 | all-reduce | flops 2048 | bytes 16384 | tf_op jit(solution)/shard_map/psum | solution.py:30
  534.3 4.9 fusion.3
  539.2 16.2 %pmax.62 = f32[1024]{0:T(1024)S(1)} all-reduce(f32[1024]{0:T(1024)S(1)} %fusion.3), channel_id=1, replica_groups=mesh['gen'=32,'beam'=8] {'beam'}, use_global_device_ids=true, to_apply=%region_27.0 | all-reduce | flops 1024 | bytes 8192 | tf_op jit(solution)/shard_map/pmax | solution.py:23
  555.4 5.1 exponential_reduce_fusion.1
  560.5 14.2 %psum.69 = f32[1024]{0:T(1024)S(1)} all-reduce(f32[1024]{0:T(1024)S(1)} %exponential_reduce_fusion.1), channel_id=1, replica_groups=mesh['gen'=32,'beam'=8] {'beam'}, use_global_device_ids=true, to_apply=%region_29.0 | all-reduce | flops 1024 | bytes 8192 | tf_op jit(solution)/shard_map/psum | solution.py:24
  580.0 63.7 %pmax.63 = f32[2048]{0:T(1024)S(1)} all-reduce(f32[2048]{0:T(1024)S(1)} %fusion.18), channel_id=1, replica_groups=mesh['gen'=32,'beam'=8] {'gen'}, use_global_device_ids=true, to_apply=%region_31.0 | all-reduce | flops 2048 | bytes 16384 | tf_op jit(solution)/shard_map/pmax | solution.py:29
  643.7 5.2 exponential_reduce_fusion
  648.9 63.7 %psum.70 = f32[2048]{0:T(1024)S(1)} all-reduce(f32[2048]{0:T(1024)S(1)} %exponential_reduce_fusion), channel_id=1, replica_groups=mesh['gen'=32,'beam'=8] {'gen'}, use_global_device_ids=true, to_apply=%region_33.0 | all-reduce | flops 2048 | bytes 16384 | tf_op jit(solution)/shard_map/psum | solution.py:30
  713.3 5.7 fusion.37
  728.0 92.3 %reduce-scatter.5.cloned.1.call-done = f32[64,128]{1,0:T(8,128)} async-done(((f32[2048,128]{1,0:T(8,128)}), f32[64,128]{1,0:T(8,128)}) %reduce-scatter.5.cloned.1.call-update) | async-done | bytes 32784 | tf_op jit(solution)/shard_map/reduce_scatter | solution.py:85
  821.3 38.7 %reduce-scatter.3.cloned.1.call-done = f32[128,128]{0,1:T(8,128)} async-done(((f32[1024,128]{0,1:T(8,128)}), f32[128,128]{0,1:T(8,128)}) %reduce-scatter.3.cloned.1.call-update) | async-done | bytes 65552 | tf_op jit(solution)/shard_map/reduce_scatter | solution.py:72
  861.7 244.8 %all-reduce.2.cloned.1.call-done = f32[256,128]{1,0:T(8,128)} async-done(((f32[256,128]{1,0:T(8,128)}), f32[256,128]{1,0:T(8,128)}) %all-reduce.2.cloned.1.call-update) | async-done | bytes 131088 | tf_op jit(solution)/shard_map/psum | solution.py:95
  (34 shorter events, 41.2 us)
Async XLA Ops:
  7.2 1.5 copy-start
  7.2 813.0 %reduce-scatter.5.cloned.1.call-start = ((), (), s32[]{:S(2)}) async-start(), calls=%async_computation.3 | async-start | bytes 1081344 | tf_op jit(solution)/shard_map/reduce_scatter | solution.py:85
  575.4 137.9 %copy-start.2 = (f32[1024]{0:T(1024)}, f32[1024]{0:T(1024)S(1)}, u32[]{:S(2)}) copy-start(f32[1024]{0:T(1024)S(1)} %subtract_multiply_fusion.4) | copy-start | bytes 12292
  713.3 10.0 copy-start.3
  719.0 1.9 copy-start.1
  723.3 136.6 %reduce-scatter.3.cloned.1.call-start = ((), (), s32[]{:S(2)}) async-start(), calls=%async_computation.2 | async-start | bytes 589824 | tf_op jit(solution)/shard_map/reduce_scatter | solution.py:72
  727.9 378.6 %all-reduce.2.cloned.1.call-start = ((), (), s32[]{:S(2)}) async-start(), calls=%async_computation.4 | async-start | bytes 262144 | tf_op jit(solution)/shard_map/psum | solution.py:95
Sparse Core Ops, SparseCore 0:
  723.5 96.7 reduce-scatter.4
  822.9 36.9 reduce-scatter.2
  866.0 240.4 all-reduce.1
where the time goes:
time: 1120 us; the launch traced here: 1110 us
  blocking collectives  617 us (55%)
  waiting for transfers between devices  376 us (34%)
  other arithmetic  85 us (8%)
  matrix products  17.8 us (2%)
  between operations  14 us (1%)
    psum x4, blocking collectives, col_lse(): total = lax.psum(jnp.sum(jnp.exp(scores - top[None, :]), axis=0), 'gen')  247 us
    pmax x4, blocking collectives, col_lse(): top = lax.pmax(jnp.max(scores, axis=0), 'gen')  245 us
    psum x1, waiting for transfers between devices, on_device(): weight_grad = lax.psum(partial_grad, ('gen', 'beam'))  245 us
    reduce_scatter x1, waiting for transfers between devices, on_device(): lax.psum_scatter(2.0 * (col_mass[:, None] * own - moved), 'gen', scatter_...  92.3 us
    pmax x4, blocking collectives, row_lse(): top = lax.pmax(jnp.max(scores, axis=1), 'beam')  68.5 us
    psum x4, blocking collectives, row_lse(): total = lax.psum(jnp.sum(jnp.exp(scores - top[:, None]), axis=1), 'beam')  56.8 us
    reduce_scatter x1, waiting for transfers between devices, on_device(): lax.psum_scatter(2.0 * (row_mass[:, None] * own - moved), 'beam', scatter...  38.7 us
  transfers between devices with their start and end apart: 3, of which 3 were waited for; matrix products, arithmetic and copies ran while one was open for 0% of the time, Pallas kernels for 0%

commit v1 on v0

--- a/solution.py
+++ b/solution.py
@@ -27,7 +27,7 @@
 
 def col_lse(scores):
     top = lax.pmax(jnp.max(scores, axis=0), "gen")
-    total = lax.psum(jnp.sum(jnp.exp(scores - top[None, :]), axis=0), "gen")
+    total = jnp.sum(lax.all_gather(jnp.sum(jnp.exp(scores - top[None, :]), axis=0), "gen"), axis=0)
     return top + jnp.log(total)
 
 

time: 1120 us -> 954 us (0.85)
  blocking collectives: 617 us -> 468 us
  waiting for transfers between devices: 376 us -> 361 us
    psum x4 -> x0, blocking collectives: 247 us -> none  [col_lse(): total = lax.psum(jnp.sum(jnp.exp(scores - top[None, :]), axis=0), 'gen')]
    all_gather x0 -> x4, blocking collectives: none -> 127 us  [col_lse(): lax.all_gather(jnp.sum(jnp.exp(scores - top[None, :]), axis=0), 'gen')]
    pmax x4, blocking collectives: 245 us -> 216 us  [col_lse(): top = lax.pmax(jnp.max(scores, axis=0), 'gen')]
    reduce_scatter x1, waiting for transfers between devices: 92.3 us -> 77.4 us  [on_device(): lax.psum_scatter(2.0 * (col_mass[:, None] * own - moved), 'gen', scatter_...]
  transfers between devices with their start and end apart: 3 -> 3, of which waited for: 3 -> 3; matrix products, arithmetic and copies ran while one was open for 0% -> 1% of each run, Pallas kernels for 0% -> 0%
where the time goes in v1:
time: 954 us; the launch traced here: 953 us
  blocking collectives  468 us (49%)
  waiting for transfers between devices  361 us (38%)
  other arithmetic  85.5 us (9%)
  matrix products  18.7 us (2%)
  between operations  14 us (1%)
    psum x1, waiting for transfers between devices, on_device(): weight_grad = lax.psum(partial_grad, ('gen', 'beam'))  245 us
    pmax x4, blocking collectives, col_lse(): top = lax.pmax(jnp.max(scores, axis=0), 'gen')  216 us
    all_gather x4, blocking collectives, col_lse(): lax.all_gather(jnp.sum(jnp.exp(scores - top[None, :]), axis=0), 'gen')  127 us
    reduce_scatter x1, waiting for transfers between devices, on_device(): lax.psum_scatter(2.0 * (col_mass[:, None] * own - moved), 'gen', scatter_...  77.4 us
    pmax x4, blocking collectives, row_lse(): top = lax.pmax(jnp.max(scores, axis=1), 'beam')  68.5 us
    psum x4, blocking collectives, row_lse(): total = lax.psum(jnp.sum(jnp.exp(scores - top[:, None]), axis=1), 'beam')  56.7 us
    reduce_scatter x1, waiting for transfers between devices, on_device(): lax.psum_scatter(2.0 * (row_mass[:, None] * own - moved), 'beam', scatter...  38.7 us
    reduce_sum x4, other arithmetic, col_lse(): jnp.sum(jnp.exp(scores - top[None, :]), axis=0)  20.6 us
  transfers between devices with their start and end apart: 3, of which 3 were waited for; matrix products, arithmetic and copies ran while one was open for 1% of the time, Pallas kernels for 0%

profile of v1, /device:TPU:8, one launch (start us, length us, event | category | flops | bytes accessed | tf_op | source)
XLA Modules:
  0.0 952.5 jit_solution(18185014976563367344)
XLA Ops:
  12.2 5.3 fusion
  17.5 20.0 %pmax.56 = f32[1024]{0:T(1024)S(1)} all-reduce(f32[1024]{0:T(1024)S(1)} %get-tuple-element.16), channel_id=1, replica_groups=mesh['gen'=32,'beam'=8] {'beam'}, use_global_device_ids=true, to_apply=%region_3.0 | all-reduce | flops 1024 | bytes 8192 | tf_op jit(solution)/shard_map/pmax | solution.py:23
  37.5 5.1 exponential_reduce_fusion.7
  42.7 14.2 %psum.35 = f32[1024]{0:T(1024)S(1)} all-reduce(f32[1024]{0:T(1024)S(1)} %exponential_reduce_fusion.7), channel_id=1, replica_groups=mesh['gen'=32,'beam'=8] {'beam'}, use_global_device_ids=true, to_apply=%region_5.0 | all-reduce | flops 1024 | bytes 8192 | tf_op jit(solution)/shard_map/psum | solution.py:24
  62.2 54.0 %pmax.57 = f32[2048]{0:T(1024)S(1)} all-reduce(f32[2048]{0:T(1024)S(1)} %fusion.15), channel_id=1, replica_groups=mesh['gen'=32,'beam'=8] {'gen'}, use_global_device_ids=true, to_apply=%region_7.0 | all-reduce | flops 2048 | bytes 16384 | tf_op jit(solution)/shard_map/pmax | solution.py:29
  116.2 5.2 exponential_reduce_fusion.6
  121.4 31.9 %all-gather = f32[65536]{0:T(1024)S(1)} all-gather(f32[2048]{0:T(1024)S(1)} %exponential_reduce_fusion.6), channel_id=2, replica_groups=mesh['gen'=32,'beam'=8] {'gen'}, dimensions={0}, use_global_device_ids=true | all-gather | bytes 270336 | tf_op jit(solution)/shard_map/all_gather | solution.py:30
  154.0 4.9 fusion.1
  158.9 16.2 %pmax.58 = f32[1024]{0:T(1024)S(1)} all-reduce(f32[1024]{0:T(1024)S(1)} %fusion.1), channel_id=1, replica_groups=mesh['gen'=32,'beam'=8] {'beam'}, use_global_device_ids=true, to_apply=%region_11.0 | all-reduce | flops 1024 | bytes 8192 | tf_op jit(solution)/shard_map/pmax | solution.py:23
  175.1 5.1 exponential_reduce_fusion.5
  180.2 14.2 %psum.36 = f32[1024]{0:T(1024)S(1)} all-reduce(f32[1024]{0:T(1024)S(1)} %exponential_reduce_fusion.5), channel_id=1, replica_groups=mesh['gen'=32,'beam'=8] {'beam'}, use_global_device_ids=true, to_apply=%region_13.0 | all-reduce | flops 1024 | bytes 8192 | tf_op jit(solution)/shard_map/psum | solution.py:24
  199.7 54.0 %pmax.59 = f32[2048]{0:T(1024)S(1)} all-reduce(f32[2048]{0:T(1024)S(1)} %fusion.16), channel_id=1, replica_groups=mesh['gen'=32,'beam'=8] {'gen'}, use_global_device_ids=true, to_apply=%region_15.0 | all-reduce | flops 2048 | bytes 16384 | tf_op jit(solution)/shard_map/pmax | solution.py:29
  253.7 5.1 exponential_reduce_fusion.4
  258.9 31.7 %all-gather.1 = f32[65536]{0:T(1024)S(1)} all-gather(f32[2048]{0:T(1024)S(1)} %exponential_reduce_fusion.4), channel_id=3, replica_groups=mesh['gen'=32,'beam'=8] {'gen'}, dimensions={0}, use_global_device_ids=true | all-gather | bytes 270336 | tf_op jit(solution)/shard_map/all_gather | solution.py:30
  291.3 4.9 fusion.2
  296.2 16.2 %pmax.60 = f32[1024]{0:T(1024)S(1)} all-reduce(f32[1024]{0:T(1024)S(1)} %fusion.2), channel_id=1, replica_groups=mesh['gen'=32,'beam'=8] {'beam'}, use_global_device_ids=true, to_apply=%region_19.0 | all-reduce | flops 1024 | bytes 8192 | tf_op jit(solution)/shard_map/pmax | solution.py:23
  312.4 5.1 exponential_reduce_fusion.3
  317.5 14.2 %psum.37 = f32[1024]{0:T(1024)S(1)} all-reduce(f32[1024]{0:T(1024)S(1)} %exponential_reduce_fusion.3), channel_id=1, replica_groups=mesh['gen'=32,'beam'=8] {'beam'}, use_global_device_ids=true, to_apply=%region_21.0 | all-reduce | flops 1024 | bytes 8192 | tf_op jit(solution)/shard_map/psum | solution.py:24
  337.0 54.0 %pmax.61 = f32[2048]{0:T(1024)S(1)} all-reduce(f32[2048]{0:T(1024)S(1)} %fusion.17), channel_id=1, replica_groups=mesh['gen'=32,'beam'=8] {'gen'}, use_global_device_ids=true, to_apply=%region_23.0 | all-reduce | flops 2048 | bytes 16384 | tf_op jit(solution)/shard_map/pmax | solution.py:29
  391.0 5.2 exponential_reduce_fusion.2
  396.2 31.5 %all-gather.2 = f32[65536]{0:T(1024)S(1)} all-gather(f32[2048]{0:T(1024)S(1)} %exponential_reduce_fusion.2), channel_id=4, replica_groups=mesh['gen'=32,'beam'=8] {'gen'}, dimensions={0}, use_global_device_ids=true | all-gather | bytes 270336 | tf_op jit(solution)/shard_map/all_gather | solution.py:30
  428.5 4.9 fusion.3
  433.4 16.2 %pmax.62 = f32[1024]{0:T(1024)S(1)} all-reduce(f32[1024]{0:T(1024)S(1)} %fusion.3), channel_id=1, replica_groups=mesh['gen'=32,'beam'=8] {'beam'}, use_global_device_ids=true, to_apply=%region_27.0 | all-reduce | flops 1024 | bytes 8192 | tf_op jit(solution)/shard_map/pmax | solution.py:23
  449.6 5.1 exponential_reduce_fusion.1
  454.7 14.2 %psum.38 = f32[1024]{0:T(1024)S(1)} all-reduce(f32[1024]{0:T(1024)S(1)} %exponential_reduce_fusion.1), channel_id=1, replica_groups=mesh['gen'=32,'beam'=8] {'beam'}, use_global_device_ids=true, to_apply=%region_29.0 | all-reduce | flops 1024 | bytes 8192 | tf_op jit(solution)/shard_map/psum | solution.py:24
  474.2 54.0 %pmax.63 = f32[2048]{0:T(1024)S(1)} all-reduce(f32[2048]{0:T(1024)S(1)} %fusion.18), channel_id=1, replica_groups=mesh['gen'=32,'beam'=8] {'gen'}, use_global_device_ids=true, to_apply=%region_31.0 | all-reduce | flops 2048 | bytes 16384 | tf_op jit(solution)/shard_map/pmax | solution.py:29
  528.2 5.2 exponential_reduce_fusion
  533.4 31.7 %all-gather.3 = f32[65536]{0:T(1024)S(1)} all-gather(f32[2048]{0:T(1024)S(1)} %exponential_reduce_fusion), channel_id=5, replica_groups=mesh['gen'=32,'beam'=8] {'gen'}, dimensions={0}, use_global_device_ids=true | all-gather | bytes 270336 | tf_op jit(solution)/shard_map/all_gather | solution.py:30
  565.9 5.7 fusion.37
  580.6 77.4 %reduce-scatter.5.cloned.1.call-done = f32[64,128]{1,0:T(8,128)} async-done(((f32[2048,128]{1,0:T(8,128)}), f32[64,128]{1,0:T(8,128)}) %reduce-scatter.5.cloned.1.call-update) | async-done | bytes 32784 | tf_op jit(solution)/shard_map/reduce_scatter | solution.py:85
  659.1 38.7 %reduce-scatter.3.cloned.1.call-done = f32[128,128]{0,1:T(8,128)} async-done(((f32[1024,128]{0,1:T(8,128)}), f32[128,128]{0,1:T(8,128)}) %reduce-scatter.3.cloned.1.call-update) | async-done | bytes 65552 | tf_op jit(solution)/shard_map/reduce_scatter | solution.py:72
  699.6 244.9 %all-reduce.2.cloned.1.call-done = f32[256,128]{1,0:T(8,128)} async-done(((f32[256,128]{1,0:T(8,128)}), f32[256,128]{1,0:T(8,128)}) %all-reduce.2.cloned.1.call-update) | async-done | bytes 131088 | tf_op jit(solution)/shard_map/psum | solution.py:95
  (42 shorter events, 42.6 us)
Async XLA Ops:
  7.2 1.5 copy-start
  7.2 650.8 %reduce-scatter.5.cloned.1.call-start = ((), (), s32[]{:S(2)}) async-start(), calls=%async_computation.3 | async-start | bytes 1081344 | tf_op jit(solution)/shard_map/reduce_scatter | solution.py:85
  469.5 96.4 %copy-start.2 = (f32[1024]{0:T(1024)}, f32[1024]{0:T(1024)S(1)}, u32[]{:S(2)}) copy-start(f32[1024]{0:T(1024)S(1)} %subtract_multiply_fusion.4) | copy-start | bytes 12292
  565.9 10.0 %copy-start.3 = (f32[2048]{0:T(1024)}, f32[2048]{0:T(1024)S(1)}, u32[]{:S(2)}) copy-start(f32[2048]{0:T(1024)S(1)} %subtract_multiply_fusion) | copy-start | bytes 24580
  571.6 1.9 copy-start.1
  576.0 121.8 %reduce-scatter.3.cloned.1.call-start = ((), (), s32[]{:S(2)}) async-start(), calls=%async_computation.2 | async-start | bytes 589824 | tf_op jit(solution)/shard_map/reduce_scatter | solution.py:72
  580.6 363.9 %all-reduce.2.cloned.1.call-start = ((), (), s32[]{:S(2)}) async-start(), calls=%async_computation.4 | async-start | bytes 262144 | tf_op jit(solution)/shard_map/psum | solution.py:95
Sparse Core Ops, SparseCore 0:
  576.1 81.8 reduce-scatter.4
  660.7 36.9 reduce-scatter.2
  703.8 240.5 all-reduce.1
